TPU v7x, 256 devices: a whole 4x4x8 slice. The times are simulated.
256 devices in a mesh: seq: 32 (over z, y_lo, core), row: 2 (over y_hi), col: 4 (over x).
Axes of the slice: x: 4, y: 4 (y_hi: 2, y_lo: 2; y = y_hi * 2 + y_lo), z: 8, core: 2. Of those that a mesh axis runs over, the one named last changes fastest.
Arguments:
- activations: bfloat16 [20480, 3072], P('seq', 'col'), may hold values from -8 to 8
- qkv_weight: bfloat16 [3072, 3, 3072], P('col', None, 'row'), may hold values from -1 to 1
- grad_out: bfloat16 [20480, 3072], P('seq', ('row', 'col')), may hold values from -6 to 6
Outputs:
- attention: bfloat16 [20480, 3072], P('seq', ('row', 'col'))
- grad_input: bfloat16 [20480, 3072], P(('seq', 'row'), 'col')
All inputs are finite; a program needn't handle non-finite values.
Results may differ from a plain program's by a relative error of at most 0.007.
The roundings to bfloat16 on the way count: a program that leaves them out, or rounds other values in their place, can miss the bound.
Values may be sent and summed in bfloat16 or wider, within the bound.
A program may use at most 128 MiB of HBM per device.

v0:
```python
import jax
import jax.numpy as jnp
from jax import lax
from jax.sharding import PartitionSpec as P

HEAD = 128


def shifted(value, axis, steps):
    count = lax.axis_size(axis)
    leading, last = (max(0, -steps), min(count, count - steps))
    return lax.ppermute(value, axis, [(source, source + steps) for source in range(leading, last)])


def attend(query, keys, values, prior_keys, prior_values, upstream, has_prior):
    length = query.shape[0]
    scaling = HEAD ** (-0.5)
    all_keys = jnp.concatenate([prior_keys, keys], 0)
    all_values = jnp.concatenate([prior_values, values], 0)
    scores = (
        jnp.einsum("qhe,khe->hqk", query, all_keys, preferred_element_type=jnp.float32) * scaling
    )
    position = lax.broadcasted_iota(jnp.int32, (length, length), 0)
    column = lax.broadcasted_iota(jnp.int32, (length, length), 1)
    visible = jnp.concatenate(
        [jnp.broadcast_to(has_prior, (length, length)), position >= column], 1
    )
    scores = jnp.where(visible[None], scores, -jnp.inf)
    highest = jnp.max(scores, axis=2, keepdims=True)
    raised = jnp.exp(scores - highest)
    weights = raised / jnp.sum(raised, axis=2, keepdims=True)
    rounded = weights.astype(jnp.bfloat16)
    context = jnp.einsum("hqk,khe->qhe", rounded, all_values, preferred_element_type=jnp.float32)
    value_grad = jnp.einsum("hqk,qhe->khe", rounded, upstream, preferred_element_type=jnp.float32)
    prob_grad = jnp.einsum("qhe,khe->hqk", upstream, all_values, preferred_element_type=jnp.float32)
    row_delta = jnp.transpose(jnp.sum(upstream.astype(jnp.float32) * context, axis=2))[:, :, None]
    score_grad = (weights * (prob_grad - row_delta)).astype(jnp.bfloat16)
    query_grad = (
        jnp.einsum("hqk,khe->qhe", score_grad, all_keys, preferred_element_type=jnp.float32)
        * scaling
    )
    key_grad = (
        jnp.einsum("hqk,qhe->khe", score_grad, query, preferred_element_type=jnp.float32) * scaling
    )
    return (context, query_grad, key_grad, value_grad)


def on_device(activations, qkv_weight, grad_out):
    length = activations.shape[0]
    head_width = grad_out.shape[1]
    head_count = head_width // HEAD
    spread = lax.all_to_all(qkv_weight, "col", split_axis=2, concat_axis=0, tiled=True)
    columns = spread.reshape(spread.shape[0], 3 * head_width)
    projected = jnp.dot(
        lax.all_gather(activations, "col", axis=1, tiled=True),
        columns,
        preferred_element_type=jnp.float32,
    )
    projections = projected.astype(jnp.bfloat16).reshape(length, 3, head_width)
    prior_pair = shifted(projections[:, 1:], "seq", 1)
    has_prior = lax.axis_index("seq") > 0
    shaped = (length, head_count, HEAD)
    context, query_grad, key_grad, value_grad = attend(
        projections[:, 0].reshape(shaped),
        projections[:, 1].reshape(shaped),
        projections[:, 2].reshape(shaped),
        prior_pair[:, 0].reshape(shaped),
        prior_pair[:, 1].reshape(shaped),
        grad_out.reshape(shaped),
        has_prior,
    )
    returned = shifted(jnp.stack([key_grad[:length], value_grad[:length]], 1), "seq", -1)
    key_total = key_grad[length:] + returned[:, 0]
    value_total = value_grad[length:] + returned[:, 1]
    qkv_grad = jnp.stack([query_grad, key_total, value_total], 1).astype(jnp.bfloat16)
    qkv_grad = qkv_grad.reshape(length, 3, head_width)
    grid_rows = lax.axis_size("row")
    grid_cols = lax.axis_size("col")
    token_blocks = qkv_grad.reshape(grid_rows, length // grid_rows, 3 * head_width)
    weight_blocks = columns.reshape(grid_cols, columns.shape[0] // grid_cols, 3 * head_width)
    partials = jnp.einsum(
        "rtk,cdk->rctd", token_blocks, weight_blocks, preferred_element_type=jnp.float32
    )
    partials = partials.reshape(
        grid_rows * grid_cols * (length // grid_rows), columns.shape[0] // grid_cols
    )
    grad_input = lax.psum_scatter(partials, ("row", "col"), scatter_dimension=0, tiled=True)
    attention = context.astype(jnp.bfloat16).reshape(length, head_width)
    return (attention, grad_input.astype(jnp.bfloat16))


def solution(mesh):
    in_specs = (P("seq", "col"), P("col", None, "row"), P("seq", ("row", "col")))
    out_specs = (P("seq", ("row", "col")), P(("seq", "row"), "col"))
    return jax.shard_map(
        on_device, mesh=mesh, in_specs=in_specs, out_specs=out_specs, check_vma=False
    )
```

profile of v0, /device:TPU:1, one launch (start us, length us, event | category | flops | bytes accessed | tf_op | source)
XLA Modules:
  0.0 408.7 jit_solution(4396334476344537433)
XLA Ops:
  7.2 0.0 all-gather.2.cloned.1.call-start
  7.2 0.7 all-gather.2.cloned.1.call-update
  7.9 0.0 reduce-scatter.2.cloned.1.call-start
  7.9 14.8 %copy.53 = bf16[768,3,1536]{0,1,2:T(4,128)(2,1)} copy(bf16[768,3,1536]{2,0,1:T(8,128)(2,1)} %param.4) | data formatting | bytes 14155776 | tf_op args[1]
  22.7 139.5 %all_to_all.15 = bf16[768,3,1536]{0,1,2:T(4,128)(2,1)S(1)} all-to-all(bf16[768,3,1536]{0,1,2:T(4,128)(2,1)} %copy.53), channel_id=1, replica_groups=mesh['seq'=32,'row'=2,'col'=4] {'col'}, dimensions={2} | all-to-all | bytes 14155776 | tf_op jit(solution)/shard_map/all_to_all | solution.py:52
  162.2 3.9 copy.54
  166.1 11.3 %copy.55 = bf16[4,768,3,384]{1,0,3,2:T(4,128)(2,1)} copy(bf16[4,768,3,384]{1,3,0,2:T(8,128)(2,1)} %bitcast.77) | data formatting | bytes 14155776 | tf_op jit(solution)/shard_map/all_to_all | solution.py:52
  177.4 7.6 %copy.85 = bf16[144,8,4,768]{3,1,2,0:T(8,128)(2,1)} copy(bf16[144,8,4,768]{3,2,1,0:T(4,128)(2,1)} %bitcast.81) | data formatting | bytes 14155776
  184.9 9.1 %convolution_convert_fusion = bf16[640,1152]{1,0:T(8,128)(2,1)S(1)} fusion(bf16[640,3072]{1,0:T(8,128)(2,1)} %all-gather.2.cloned.1.call-done, bf16[3072,1152]{0,1:T(8,128)(2,1)} %bitcast.86), kind=kOutput, calls=%fused_computation.11 | convolution fusion | flops 4530585600 | bytes 12484608 | tf_op jit(solution)/shard_map/dot_general | solution.py:54
  194.0 0.9 copy.56
  195.0 1.0 slice.48
  196.0 4.9 %collective-permute-start = (bf16[640,2,384]{0,2,1:T(8,128)(2,1)}, bf16[640,2,384]{0,2,1:T(8,128)(2,1)}, u32[]{:S(2)}, u32[]{:S(2)}) collective-permute-start(bf16[640,2,384]{0,2,1:T(8,128)(2,1)} %slice.48), channel_id=1, source_target_pairs={{0,8},{8,16},{16,24},{24,32},{32,40},{40,48},{48,56},{56,64},{64,7... | collective-permute-start | bytes 2949128 | tf_op jit(solution)/shard_map/ppermute | solution.py:12
  200.9 1.3 copy.60
  202.2 0.1 iota_compare_fusion
  202.4 1.1 concatenate.10
  203.5 1.1 fusion.29
  204.6 1.5 copy.58
  206.0 0.0 copy-start.4
  206.1 6.0 %collective-permute-done = bf16[640,2,384]{0,2,1:T(8,128)(2,1)} collective-permute-done((bf16[640,2,384]{0,2,1:T(8,128)(2,1)}, bf16[640,2,384]{0,2,1:T(8,128)(2,1)}, u32[]{:S(2)}, u32[]{:S(2)}) %collective-permute-start) | collective-permute-done | bytes 983072 | tf_op jit(solution)/shard_map/ppermute | solution.py:12
  212.1 2.0 fusion.30
  214.1 0.3 copy.57
  214.4 8.6 %fusion.31 = (f32[3,640]{1,0:T(4,128)S(1)}, f32[3,640,1280]{2,1,0:T(8,128)}) fusion(pred[640,1280]{1,0:T(8,128)(4,1)} %concatenate.10, bf16[640,3,128]{0,2,1:T(8,128)(2,1)S(1)} %bitcast.90, bf16[640,3,128]{2,0,1:T(8,128)(2,1)S(1)} %copy.58, bf16[640,3,128]{2,0,1:T(8,128)(2,1)S(1)} %copy.57), kind=kOutput, calls=%fused_computation.48 | convolution fusion | flops 640943360 | bytes 12131840 | tf_op jit(solution)/shard_map/sub | solution.py:30
  223.0 4.8 %fusion.6 = bf16[3,640,1280]{2,1,0:T(8,128)(2,1)S(1)} fusion(f32[3,640,1280]{2,1,0:T(8,128)} %get-tuple-element.20, f32[3,640]{1,0:T(4,128)S(1)} %get-tuple-element.19), kind=kLoop, calls=%fused_computation.10 | loop fusion | flops 4915200 | bytes 14753280 | tf_op jit(solution)/shard_map/convert_element_type | solution.py:32
  227.8 0.0 copy-start.8
  227.8 0.0 copy-start.9
  227.9 1.0 convolution_bitcast_fusion
  228.8 0.0 copy-done.8
  228.9 0.1 copy-done.9
  229.0 2.4 multiply_reduce_fusion
  231.4 5.3 %fusion.1 = bf16[3,640,1280]{2,1,0:T(8,128)(2,1)S(1)} fusion(bf16[640,3,128]{0,2,1:T(8,128)(2,1)S(1)} %bitcast.89, f32[3,640]{1,0:T(4,128)S(1)} %bitcast.100, f32[3,640,1280]{2,1,0:T(8,128)} %get-tuple-element.20, f32[3,640]{1,0:T(4,128)S(1)} %get-tuple-element.19, bf16[640,3,128]{0,2,1:T(8,128)(2,1)S(1)} %bitcast.97, bf16[640,3,128]{0,2,1:T(8,128)(2,1)S(1)} %bitcast.99), kind=kOutput, calls=%fused_computation.2 | convolution fusion | flops 640942080 | bytes 16235520 | tf_op jit(solution)/shard_map/qhe,khe->hqk/dot_general | solution.py:35
  236.7 0.0 slice-start
  236.7 1.0 fusion.7
  237.7 1.4 copy-done
  239.1 0.1 slice_bitcast_fusion.2
  239.2 1.5 pad_maximum_fusion
  240.7 2.3 collective-permute-start.1
  243.0 3.4 copy.68
  246.4 2.7 fusion.13
  249.1 18.7 %collective-permute-done.1 = f32[640,2,3,128]{0,3,2,1:T(8,128)} collective-permute-done((f32[640,2,3,128]{0,3,2,1:T(8,128)}, f32[640,2,3,128]{0,3,2,1:T(8,128)}, u32[]{:S(2)}, u32[]{:S(2)}) %collective-permute-start.1) | collective-permute-done | bytes 1966112 | tf_op jit(solution)/shard_map/ppermute | solution.py:12
  267.8 1.7 fusion.18
  269.5 0.2 pad_maximum_fusion.1
  269.7 1.5 convert_element_type.34
  271.2 10.5 %fusion.8 = f32[2,320,4,768]{3,1,2,0:T(8,128)} fusion(bf16[4,768,1152,1]{1,2,0,3:T(8,128)(2,1)} %bitcast.85, bf16[2,320,1152,1]{1,0,2,3:T(2,128)(2,1)S(1)} %bitcast.94), kind=kOutput, calls=%fused_computation.16 | convolution fusion | flops 4529848320 | bytes 16416768 | tf_op jit(solution)/shard_map/rtk,cdk->rctd/dot_general | solution.py:81
  281.7 0.0 reduce-scatter.2.cloned.1.call-update
  281.7 1.0 copy-done.7
  282.8 1.0 copy.71
  283.7 116.1 %reduce-scatter.2.cloned.1.call-done = f32[320,768]{1,0:T(8,128)} async-done(((f32[2560,768]{1,0:T(8,128)}), f32[320,768]{1,0:T(8,128)}) %reduce-scatter.2.cloned.1.call-update) | async-done | bytes 983056 | tf_op jit(solution)/shard_map/reduce_scatter | solution.py:87
  399.8 2.0 convert_element_type.35
  (18 shorter events, 0.0 us)
Async XLA Ops:
  7.2 177.8 %all-gather.2.cloned.1.call-start = ((), (), s32[]{:S(2)}) async-start(), calls=%async_computation.2 | async-start | bytes 4915200 | tf_op jit(solution)/shard_map/all_gather | solution.py:55
  7.9 391.9 %reduce-scatter.2.cloned.1.call-start = ((), (), s32[]{:S(2)}) async-start(), calls=%async_computation.3 | async-start | bytes 8847360 | tf_op jit(solution)/shard_map/reduce_scatter | solution.py:87
  196.0 16.1 %collective-permute-start = (bf16[640,2,384]{0,2,1:T(8,128)(2,1)}, bf16[640,2,384]{0,2,1:T(8,128)(2,1)}, u32[]{:S(2)}, u32[]{:S(2)}) collective-permute-start(bf16[640,2,384]{0,2,1:T(8,128)(2,1)} %slice.48), channel_id=1, source_target_pairs={{0,8},{8,16},{16,24},{24,32},{32,40},{40,48},{48,56},{56,64},{64,7... | collective-permute-start | bytes 2949128 | tf_op jit(solution)/shard_map/ppermute | solution.py:12
  204.6 18.4 %copy-start.2 = (bf16[640,1,384]{0,2,1:T(8,128)(2,1)}, bf16[640,1,384]{0,2,1:T(8,128)(2,1)S(1)}, u32[]{:S(2)}) copy-start(bf16[640,1,384]{0,2,1:T(8,128)(2,1)S(1)} %get-tuple-element.14) | copy-start | bytes 1474564
  206.0 17.0 %copy-start.4 = (bf16[640,3,128]{2,0,1:T(8,128)(2,1)}, bf16[640,3,128]{2,0,1:T(8,128)(2,1)S(1)}, u32[]{:S(2)}) copy-start(bf16[640,3,128]{2,0,1:T(8,128)(2,1)S(1)} %copy.58) | copy-start | bytes 1474564
  214.4 8.6 %copy-start.6 = (bf16[640,3,128]{2,0,1:T(8,128)(2,1)}, bf16[640,3,128]{2,0,1:T(8,128)(2,1)S(1)}, u32[]{:S(2)}) copy-start(bf16[640,3,128]{2,0,1:T(8,128)(2,1)S(1)} %copy.57) | copy-start | bytes 1474564
  227.8 1.0 copy-start.8
  227.8 1.2 copy-start.9
  231.4 5.4 %copy-start.3 = (bf16[640,1,384]{0,2,1:T(8,128)(2,1)S(1)}, bf16[640,1,384]{0,2,1:T(8,128)(2,1)}, u32[]{:S(2)}) copy-start(bf16[640,1,384]{0,2,1:T(8,128)(2,1)} %copy-done.2) | copy-start | bytes 1474564
  236.7 6.2 %slice-start = ((s8[7077888]{0:T(1024)(128)(4,1)}), s8[4194304]{0:T(1024)(128)(4,1)S(1)}, s32[]{:S(2)}) async-start(s8[7077888]{0:T(1024)(128)(4,1)} %bitcast.78), calls=%async_computation.4 | async-start | bytes 8388608
  237.7 1.4 copy-start
  239.1 3.9 slice-start.1
  240.7 5.7 %copy-start.5 = (bf16[640,3,128]{2,0,1:T(8,128)(2,1)S(1)}, bf16[640,3,128]{2,0,1:T(8,128)(2,1)}, u32[]{:S(2)}) copy-start(bf16[640,3,128]{2,0,1:T(8,128)(2,1)} %copy-done.4) | copy-start | bytes 1474564
  240.7 27.1 %collective-permute-start.1 = (f32[640,2,3,128]{0,3,2,1:T(8,128)}, f32[640,2,3,128]{0,3,2,1:T(8,128)}, u32[]{:S(2)}, u32[]{:S(2)}) collective-permute-start(f32[640,2,3,128]{0,3,2,1:T(8,128)} %pad_maximum_fusion), channel_id=1, source_target_pairs={{8,0},{16,8},{24,16},{32,24},{40,32},{48,40},{56,48},{64,56},{72,6... | collective-permute-start | bytes 5898248 | tf_op jit(solution)/shard_map/ppermute | solution.py:12
  246.4 21.4 %copy-start.1 = (f32[1280,3,128]{0,2,1:T(8,128)S(1)}, f32[1280,3,128]{0,2,1:T(8,128)}, u32[]{:S(2)}) copy-start(f32[1280,3,128]{0,2,1:T(8,128)} %copy-done) | copy-start | bytes 5898244
  281.7 1.0 copy-start.7
Sparse Core Ops, SparseCore 0:
  9.8 109.9 all-gather.1
  281.9 117.8 reduce-scatter.1
where the time goes:
time: 410 us; the launch traced here: 409 us
  waiting for transfers between devices  142 us (35%)
  blocking collectives  139 us (34%)
  local copies, waits for them, and re-layouts  55.3 us (13%)
  matrix products  40.6 us (10%)
  between operations  14.3 us (3%)
  other arithmetic  10.3 us (3%)
  starting transfers between devices  7.25 us (2%)
    all_to_all x1, blocking collectives, on_device(): lax.all_to_all(qkv_weight, 'col', split_axis=2, concat_axis=0, tiled=True)  139 us
    reduce_scatter x1, waiting for transfers between devices, on_device(): lax.psum_scatter(partials, ('row', 'col'), scatter_dimension=0, tiled=True)  116 us
    unnamed x28, local copies, waits for them, and re-layouts  27.2 us
    ppermute x2, waiting for transfers between devices, shifted(): lax.ppermute(value, axis, [(source, source + steps) for source in range(l...  24.8 us
    all_to_all x3, local copies, waits for them, and re-layouts, on_device(): lax.all_to_all(qkv_weight, 'col', split_axis=2, concat_axis=0, tiled=True)  18.5 us
    dot_general x1, matrix products, on_device(): jnp.einsum('rtk,cdk->rctd', token_blocks, weight_blocks, preferred_elemen...  10.5 us
    dot_general x1, matrix products, on_device(): jnp.dot(lax.all_gather(activations, 'col', axis=1, tiled=True), columns,...  9.11 us
    sub x1, matrix products, attend(): raised = jnp.exp(scores - highest)  8.59 us
  transfers between devices with their start and end apart: 4, of which 3 were waited for; matrix products, arithmetic and copies ran while one was open for 12% of the time, Pallas kernels for 0%

commit v1 on v0

v1 whole, which is shorter than its diff:
```python
import functools

import jax
import jax.numpy as jnp
from jax import lax
from jax.experimental import pallas as pl
from jax.experimental.pallas import tpu as pltpu
from jax.sharding import PartitionSpec as P

HEAD = 128
HEADS = 3
LOG2E = 1.4426950408889634
MESH = pl.DeviceIdType.MESH
BF = jnp.bfloat16
F32 = jnp.float32
PLACE = (2, 0, 1)


def dot(a, b):
    return jnp.dot(a, b, preferred_element_type=F32)


def dot_nt(a, b):
    return lax.dot_general(a, b, (((1,), (1,)), ((), ())), preferred_element_type=F32)


def kernel(
    act_hbm, w_hbm, go_hbm, attn_ref, gin_ref,
    act, w, acc, go, go_t, query, pair, pair_t, prior, prior_t, own_grad, prior_grad,
    sent_grad, back_grad, grads, opp_out, opp_in, full_out, full_in, row_out, row_in,
    local_sem, inj_send, inj_recv, act_send, act_recv, z_send, z_recv, core_send, core_recv,
    kv_send, kv_recv, gr_send, gr_recv, opp_send, opp_recv, full_send, full_recv, row_send, row_recv,
):
    seq, row, col = lax.axis_index("seq"), lax.axis_index("row"), lax.axis_index("col")
    n_seq = lax.axis_size("seq")
    n_z = n_seq // 4
    z, core = seq // 4, seq % 2
    length, depth = act_hbm.shape
    width = go_hbm.shape[1]
    half = length // 2
    part = depth // (2 * n_z)

    def at_col(step):
        return (seq, row, (col + step) % 4)

    def at_seq(index):
        return (index, row, col)

    right, opposite, left = at_col(1), at_col(2), at_col(3)
    up, down = at_seq((seq + 4) % n_seq), at_seq((seq + n_seq - 4) % n_seq)
    twin = at_seq(seq + 1 - 2 * core)
    following, previous = at_seq((seq + 1) % n_seq), at_seq((seq + n_seq - 1) % n_seq)
    partner = (seq, 1 - row, col)

    def remote(src, dst, send, recv, device):
        return pltpu.make_async_remote_copy(
            src_ref=src, dst_ref=dst, send_sem=send, recv_sem=recv, device_id=device, device_id_type=MESH
        )

    own_cols = pl.ds(pl.multiple_of(col * width, 128), width)
    locals_ = [pltpu.make_async_copy(act_hbm, act.at[0], local_sem.at[0])]
    for kind in range(3):
        at = PLACE[kind] * width
        locals_.append(
            pltpu.make_async_copy(w_hbm.at[kind, :, own_cols], w.at[0, :, at : at + width], local_sem.at[1 + kind])
        )
    for head in range(HEADS):
        locals_.append(
            pltpu.make_async_copy(
                go_hbm.at[:, head * HEAD : (head + 1) * HEAD], go.at[head], local_sem.at[4 + head]
            )
        )
    for copy in locals_:
        copy.start()

    barrier = pltpu.get_barrier_semaphore()
    friends = (right, opposite, left, up, down, twin, following, previous, partner)
    for friend in friends:
        pl.semaphore_signal(barrier, inc=1, device_id=friend, device_id_type=MESH)
    pl.semaphore_wait(barrier, len(friends))

    def rows_of(z_at, core_at):
        return pl.ds(pl.multiple_of(z_at * (2 * part) + core_at * part, 16), part)

    mine = rows_of(z, core)
    injections = []
    for step in (2, 1, 3):
        cols = pl.ds(pl.multiple_of(((col + step) % 4) * width, 128), width)
        for kind in range(3):
            at = PLACE[kind] * width
            injections.append(
                remote(
                    w_hbm.at[kind, mine, cols],
                    w.at[4 - step, mine, at : at + width],
                    inj_send.at[4 - step, kind],
                    inj_recv.at[4 - step, kind],
                    at_col(step),
                )
            )
    for copy in injections:
        copy.start()

    top, bottom = pl.ds(0, half), pl.ds(half, half)
    act_copies = [
        remote(act_hbm.at[top], act.at[3, top], act_send.at[0], act_recv.at[0], right),
        remote(act_hbm.at[bottom], act.at[1, bottom], act_send.at[1], act_recv.at[1], left),
        remote(act_hbm.at[bottom], act.at[3, bottom], act_send.at[2], act_recv.at[2], right),
        remote(act_hbm.at[top], act.at[1, top], act_send.at[3], act_recv.at[3], left),
        remote(act.at[3, top], act.at[2, top], act_send.at[4], act_recv.at[4], right),
        remote(act.at[1, bottom], act.at[2, bottom], act_send.at[5], act_recv.at[5], left),
    ]
    for copy in act_copies[:4]:
        copy.start()

    for copy in locals_[:4]:
        copy.wait()

    def project(index, first):
        @pl.loop(0, 2)
        def _(i):
            rows = pl.ds(pl.multiple_of(i * half, half), half)
            term = dot(act[index, rows, :], w[index])
            acc[rows, :] = term if first else acc[rows, :] + term

    project(0, True)
    for copy in locals_[4:]:
        copy.wait()
    for head in range(HEADS):
        go_t[head] = jnp.transpose(go[head])

    for copy in injections:
        copy.wait_recv()
    cut = 640
    total = 3 * width

    def ring(way, step):
        origin = (z + n_z - step) % n_z if way == 0 else (z + step) % n_z
        rows = rows_of(origin, core)
        if step < n_z // 2 - 1:
            block = w.at[1:4, rows, :]
        else:
            block = w.at[1:4, rows, 0:cut] if way == 0 else w.at[1:4, rows, cut:total]
        return remote(block, block, z_send.at[way, step], z_recv.at[way, step], (up, down)[way])

    def across(index, origin):
        block = w.at[1:4, rows_of(origin, core), :]
        return remote(block, block, core_send.at[index], core_recv.at[index], twin)

    steps = n_z // 2
    rings = [[ring(way, step) for way in (0, 1)] for step in range(steps)]
    acrosses = [across(0, z)]
    for step in range(1, steps):
        acrosses.append(across(2 * step - 1, (z + n_z - step) % n_z))
        acrosses.append(across(2 * step, (z + step) % n_z))
    acrosses.append(across(2 * steps - 1, (z + steps) % n_z))
    for copy in rings[0]:
        copy.start()
    acrosses[0].start()
    for step in range(1, steps):
        for way in (0, 1):
            rings[step - 1][way].wait_recv()
            rings[step][way].start()
            acrosses[2 * step - 1 + way].start()
        if step == 1:
            for i in (0, 1):
                act_copies[i].wait_recv()
                act_copies[4 + i].start()
    for way in (0, 1):
        rings[steps - 1][way].wait_recv()
    acrosses[-1].start()
    for copy in acrosses:
        copy.wait_recv()
    for i in (2, 3):
        act_copies[i].wait_recv()
    project(1, False)
    project(3, False)
    for i in (4, 5):
        act_copies[i].wait_recv()

    for i in range(2):
        rows = pl.ds(i * half, half)
        done = (acc[rows, 0 : 2 * width] + dot(act[2, rows, :], w[2, :, 0 : 2 * width])).astype(BF)
        for head in range(HEADS):
            for kind in range(2):
                at = kind * width + head * HEAD
                pair[head, kind, rows, :] = done[:, at : at + HEAD]
    kv_copies = [
        remote(pair.at[head], prior.at[head], kv_send.at[head], kv_recv.at[head], following) for head in range(HEADS)
    ]
    for copy in kv_copies:
        copy.start()
    for i in range(2):
        rows = pl.ds(i * half, half)
        done = (acc[rows, 2 * width : total] + dot(act[2, rows, :], w[2, :, 2 * width : total])).astype(BF)
        for head in range(HEADS):
            query[head, rows, :] = done[:, head * HEAD : (head + 1) * HEAD]
    for head in range(HEADS):
        for kind in range(2):
            pair_t[head, kind] = jnp.transpose(pair[head, kind])

    scaling = HEAD**-0.5
    base = scaling * LOG2E
    has_prior = seq > 0

    gr_copies = [
        remote(sent_grad.at[head], back_grad.at[head], gr_send.at[head], gr_recv.at[head], previous)
        for head in range(HEADS)
    ]

    for head in range(HEADS):
        kv_copies[head].wait_recv()
        for kind in range(2):
            prior_t[kind] = jnp.transpose(prior[head, kind])
        prior_keys, prior_values = prior[head, 0], prior[head, 1]
        for q0, size in ((0, 256), (256, 256), (512, 128)):
            seen = q0 + size
            q_t = query[head, q0:seen, :]
            up_q = go[head, q0:seen, :]
            s_own = dot_nt(pair[head, 0, 0:seen, :], q_t)
            s_prior = dot_nt(prior_keys, q_t)
            key_at = lax.broadcasted_iota(jnp.int32, (seen, size), 0)
            query_at = lax.broadcasted_iota(jnp.int32, (seen, size), 1) + q0
            s_own = jnp.where(key_at <= query_at, s_own, -jnp.inf)
            top_prior = jnp.where(has_prior, jnp.max(s_prior, axis=0, keepdims=True), -jnp.inf)
            highest = jnp.maximum(jnp.max(s_own, axis=0, keepdims=True), top_prior) * base
            e_own = jnp.exp2(s_own * base - highest)
            e_prior = jnp.exp2(s_prior * base - jnp.where(has_prior, highest, jnp.inf))
            inverse = 1.0 / (jnp.sum(e_own, axis=0, keepdims=True) + jnp.sum(e_prior, axis=0, keepdims=True))
            w_own, w_prior = e_own * inverse, e_prior * inverse
            p_own, p_prior = w_own.astype(BF), w_prior.astype(BF)
            ctx_t = dot(prior_t[1], p_prior) + dot(pair_t[head, 1, :, 0:seen], p_own)
            delta = jnp.sum(go_t[head, :, q0:seen].astype(F32) * ctx_t, axis=0, keepdims=True)
            attn_ref[q0:seen, head * HEAD : (head + 1) * HEAD] = jnp.transpose(ctx_t).astype(BF)
            ds_own = (w_own * (dot_nt(pair[head, 1, 0:seen, :], up_q) - delta)).astype(BF)
            ds_prior = (w_prior * (dot_nt(prior_values, up_q) - delta)).astype(BF)
            dq_t = dot(prior_t[0], ds_prior) + dot(pair_t[head, 0, :, 0:seen], ds_own)
            at = 2 * width + head * HEAD
            grads[q0:seen, at : at + HEAD] = (jnp.transpose(dq_t) * scaling).astype(BF)
            terms = (dot(ds_own, q_t), dot(p_own, up_q))
            prior_terms = (dot(ds_prior, q_t), dot(p_prior, up_q))
            for kind in range(2):
                if q0:
                    own_grad[head, kind, 0:q0, :] = own_grad[head, kind, 0:q0, :] + terms[kind][0:q0]
                    prior_grad[kind] = prior_grad[kind] + prior_terms[kind]
                else:
                    prior_grad[kind] = prior_terms[kind]
                own_grad[head, kind, q0:seen, :] = terms[kind][q0:seen]
        sent_grad[head, 0] = (prior_grad[0] * scaling).astype(BF)
        sent_grad[head, 1] = prior_grad[1].astype(BF)
        gr_copies[head].start()

    for head in range(HEADS):
        gr_copies[head].wait_recv()
        for kind in range(2):
            at = kind * width + head * HEAD
            own = own_grad[head, kind]
            own = own * scaling if kind == 0 else own
            grads[:, at : at + HEAD] = (own + back_grad[head, kind].astype(F32)).astype(BF)

    halves = [pl.ds(pl.multiple_of((1 - row) * half, half), half), pl.ds(pl.multiple_of(row * half, half), half)]
    mid = depth // 2

    def share(index, which):
        return dot_nt(grads[halves[which], :], w[index])

    opp_copies, full_copies = [], []
    for which in (0, 1):
        for way in (0, 1):
            opp_copies.append(
                remote(
                    opp_out.at[way, which], opp_in.at[way, which], opp_send.at[way, which], opp_recv.at[way, which],
                    (right, left)[way],
                )
            )
            full_copies.append(
                remote(
                    full_out.at[way, which], full_in.at[way, which], full_send.at[way, which],
                    full_recv.at[way, which], (right, left)[way],
                )
            )
    for which in (0, 1):
        term = share(2, which).astype(BF)
        opp_out[0, which] = term[:, mid:]
        opp_out[1, which] = term[:, :mid]
        for way in (0, 1):
            opp_copies[2 * which + way].start()
    for which in (0, 1):
        for way in (0, 1):
            term = share((1, 3)[way], which)
            opp_copies[2 * which + way].wait_recv()
            arrived = opp_in[way, which].astype(F32)
            if way == 0:
                full_out[way, which, :, :mid] = term[:, :mid].astype(BF)
                full_out[way, which, :, mid:] = (term[:, mid:] + arrived).astype(BF)
            else:
                full_out[way, which, :, :mid] = (term[:, :mid] + arrived).astype(BF)
                full_out[way, which, :, mid:] = term[:, mid:].astype(BF)
            full_copies[2 * which + way].start()
    row_copy = remote(row_out, row_in, row_send, row_recv, partner)
    for which in (0, 1):
        term = share(0, which)
        for way in (0, 1):
            full_copies[2 * which + way].wait_recv()
            term = term + full_in[way, which].astype(F32)
        if which == 0:
            row_out[...] = term.astype(BF)
            row_copy.start()
        else:
            row_copy.wait_recv()
            gin_ref[...] = (term + row_in[...].astype(F32)).astype(BF)

    for copy in injections + act_copies + [c for pair_ in rings for c in pair_] + acrosses:
        copy.wait_send()
    for copy in kv_copies + gr_copies + opp_copies + full_copies + [row_copy]:
        copy.wait_send()


def on_device(activations, qkv_weight, grad_out):
    length, depth = activations.shape
    width = grad_out.shape[1]
    half = length // 2
    steps = lax.axis_size("seq") // 8
    weights = jnp.transpose(qkv_weight, (1, 0, 2))
    anywhere = pl.BlockSpec(memory_space=pl.ANY)
    vmem = pl.BlockSpec(memory_space=pltpu.VMEM)
    dma = pltpu.SemaphoreType.DMA
    return pl.pallas_call(
        kernel,
        out_shape=(
            jax.ShapeDtypeStruct((length, width), BF),
            jax.ShapeDtypeStruct((half, depth), BF),
        ),
        in_specs=[anywhere] * 3,
        out_specs=(vmem, vmem),
        scratch_shapes=[
            pltpu.VMEM((4, length, depth), BF),
            pltpu.VMEM((4, depth, 3 * width), BF),
            pltpu.VMEM((length, 3 * width), F32),
            pltpu.VMEM((HEADS, length, HEAD), BF),
            pltpu.VMEM((HEADS, HEAD, length), BF),
            pltpu.VMEM((HEADS, length, HEAD), BF),
            pltpu.VMEM((HEADS, 2, length, HEAD), BF),
            pltpu.VMEM((HEADS, 2, HEAD, length), BF),
            pltpu.VMEM((HEADS, 2, length, HEAD), BF),
            pltpu.VMEM((2, HEAD, length), BF),
            pltpu.VMEM((HEADS, 2, length, HEAD), F32),
            pltpu.VMEM((2, length, HEAD), F32),
            pltpu.VMEM((HEADS, 2, length, HEAD), BF),
            pltpu.VMEM((HEADS, 2, length, HEAD), BF),
            pltpu.VMEM((length, 3 * width), BF),
            pltpu.VMEM((2, 2, half, depth // 2), BF),
            pltpu.VMEM((2, 2, half, depth // 2), BF),
            pltpu.VMEM((2, 2, half, depth), BF),
            pltpu.VMEM((2, 2, half, depth), BF),
            pltpu.VMEM((half, depth), BF),
            pltpu.VMEM((half, depth), BF),
            dma((7,)),
            dma((4, 3)),
            dma((4, 3)),
            dma((6,)),
            dma((6,)),
            dma((2, steps)),
            dma((2, steps)),
            dma((2 * steps,)),
            dma((2 * steps,)),
            dma((HEADS,)),
            dma((HEADS,)),
            dma((HEADS,)),
            dma((HEADS,)),
            dma((2, 2)),
            dma((2, 2)),
            dma((2, 2)),
            dma((2, 2)),
            dma,
            dma,
        ],
        compiler_params=pltpu.CompilerParams(
            collective_id=0, has_side_effects=True, vmem_limit_bytes=60 * 2**20
        ),
    )(activations, weights, grad_out)


def solution(mesh):
    in_specs = (P("seq", "col"), P("col", None, "row"), P("seq", ("row", "col")))
    out_specs = (P("seq", ("row", "col")), P(("seq", "row"), "col"))
    return jax.shard_map(on_device, mesh=mesh, in_specs=in_specs, out_specs=out_specs, check_vma=False)
```

time: 410 us -> 119 us (0.29)
  waiting for transfers between devices: 142 us -> 0 us
  blocking collectives: 139 us -> 0 us
  Pallas kernels: 0 us -> 114 us
  local copies, waits for them, and re-layouts: 55.3 us -> 3.7 us
  matrix products: 40.6 us -> 0 us
  between operations: 14.3 us -> 0.64 us
  other arithmetic: 10.3 us -> 0 us
  starting transfers between devices: 7.25 us -> 0 us
    all_to_all x1 -> x0, blocking collectives: 139 us -> none  [on_device(): lax.all_to_all(qkv_weight, 'col', split_axis=2, concat_axis=0, tiled=True)]
    reduce_scatter x1 -> x0, waiting for transfers between devices: 116 us -> none  [on_device(): lax.psum_scatter(partials, ('row', 'col'), scatter_dimension=0, tiled=True)]
    pallas_call x0 -> x1, Pallas kernels: none -> 114 us  [on_device(): pl.pallas_call(kernel, out_shape=(jax.ShapeDtypeStruct((length, width), B...]
    dot_general x7 -> x0, matrix products: 32 us -> none  [the longest x1 10.5 us: on_device(): jnp.einsum('rtk,cdk->rctd', token_blocks, weight_blocks, preferred_elemen...]
    ppermute x2 -> x0, waiting for transfers between devices: 24.8 us -> none  [shifted(): lax.ppermute(value, axis, [(source, source + steps) for source in range(l...]
    unnamed x28 -> x2, local copies, waits for them, and re-layouts: 27.2 us -> 3.7 us
    all_to_all x3 -> x0, local copies, waits for them, and re-layouts: 18.5 us -> none  [on_device(): lax.all_to_all(qkv_weight, 'col', split_axis=2, concat_axis=0, tiled=True)]
    sub x1 -> x0, matrix products: 8.59 us -> none  [attend(): raised = jnp.exp(scores - highest)]
  transfers between devices with their start and end apart: 4 -> 0, of which waited for: 3 -> 0; matrix products, arithmetic and copies ran while one was open for 12% -> 0% of each run, Pallas kernels for 0% -> 0%
where the time goes in v1:
time: 119 us
  Pallas kernels  114 us (96%)
  local copies, waits for them, and re-layouts  3.7 us (3%)
    pallas_call x1, Pallas kernels, on_device(): pl.pallas_call(kernel, out_shape=(jax.ShapeDtypeStruct((length, width), B...  114 us
    unnamed x2, local copies, waits for them, and re-layouts  3.7 us

profile of v1, /device:TPU:1, one launch (start us, length us, event | category | flops | bytes accessed | tf_op | source)
XLA Modules:
  0.0 118.6 jit_solution(3191205983204234999)
XLA Ops:
  0.6 114.3 %shard_map.50 = (bf16[640,384]{1,0:T(8,128)(2,1)}, bf16[320,768]{1,0:T(8,128)(2,1)}) custom-call(bf16[640,768]{1,0:T(8,128)(2,1)} %act_hbm.1, bf16[3,768,1536]{2,1,0:T(8,128)(2,1)} %bitcast.1, bf16[640,384]{1,0:T(8,128)(2,1)} %go_hbm.1), custom_call_target="tpu_custom_call" | custom-call | tf_op jit(solution)/shard_map/pallas_call | solution.py:327
  114.9 1.9 %copy.7 = bf16[640,384]{1,0:T(8,128)(2,1)} copy(bf16[640,384]{1,0:T(8,128)(2,1)} %get-tuple-element.4) | data formatting | bytes 983040
  116.8 1.8 %copy.8 = bf16[320,768]{1,0:T(8,128)(2,1)} copy(bf16[320,768]{1,0:T(8,128)(2,1)} %get-tuple-element.5) | data formatting | bytes 983040

commit v2 on v1

v2 whole, which is shorter than its diff:
```python
import functools

import jax
import jax.numpy as jnp
from jax import lax
from jax.experimental import pallas as pl
from jax.experimental.pallas import tpu as pltpu
from jax.sharding import PartitionSpec as P

HEAD = 128
HEADS = 3
GROUPS = 4
TILES = ((256, 256), (512, 256), (640, 128))
LOG2E = 1.4426950408889634
MESH = pl.DeviceIdType.MESH
BF = jnp.bfloat16
F32 = jnp.float32
PLACE = (2, 0, 1)


def dot(a, b):
    return jnp.dot(a, b, preferred_element_type=F32)


def dot_nt(a, b):
    return lax.dot_general(a, b, (((1,), (1,)), ((), ())), preferred_element_type=F32)


def kernel(
    act_hbm, w_hbm, go_hbm, attn_ref, gin_ref,
    act, w, acc, go, go_t, query, pair, pair_t, prior, prior_t,
    s_a, s_b, s_c, dp_a, dp_b, dp_c, p_a, p_b, p_c, ds_a, ds_b, ds_c, p_prior, ds_prior,
    own_grad, sent_grad, back_grad, grads, cross_out, cross_in, opp_out, opp_in, full_out, full_in, row_out, row_in,
    local_sem, inj_send, inj_recv, act_send, act_recv, fwd_send, fwd_recv, swap_send, swap_recv,
    z_send, z_recv, y_send, y_recv, core_send, core_recv, kv_send, kv_recv, gr_send, gr_recv,
    cross_send, cross_recv, opp_send, opp_recv, full_send, full_recv, row_send, row_recv,
):
    seq, row, col = lax.axis_index("seq"), lax.axis_index("row"), lax.axis_index("col")
    n_seq = lax.axis_size("seq")
    n_z = n_seq // 4
    z, side, core = seq // 4, (seq // 2) % 2, seq % 2
    length, depth = act_hbm.shape
    width = go_hbm.shape[1]
    total = 3 * width
    half = length // 2
    group = length // GROUPS
    part = depth // (2 * n_z)

    def at_col(step):
        return (seq, row, (col + step) % 4)

    def at_seq(index):
        return (index, row, col)

    right, opposite, left = at_col(1), at_col(2), at_col(3)
    up, down = at_seq((seq + 4) % n_seq), at_seq((seq + n_seq - 4) % n_seq)
    twin = at_seq(seq + 1 - 2 * core)
    beside = at_seq(seq + 2 - 4 * side)
    following, previous = at_seq((seq + 1) % n_seq), at_seq((seq + n_seq - 1) % n_seq)
    partner = (seq, 1 - row, col)
    sent = []

    def remote(src, dst, send, recv, device):
        return pltpu.make_async_remote_copy(
            src_ref=src, dst_ref=dst, send_sem=send, recv_sem=recv, device_id=device, device_id_type=MESH
        )

    def start(copy):
        copy.start()
        sent.append(copy)

    own_cols = pl.ds(pl.multiple_of(col * width, 128), width)
    locals_ = [pltpu.make_async_copy(act_hbm, act.at[0], local_sem.at[0])]
    for kind in range(3):
        at = PLACE[kind] * width
        locals_.append(
            pltpu.make_async_copy(w_hbm.at[kind, :, own_cols], w.at[0, :, at : at + width], local_sem.at[1 + kind])
        )
    for head in range(HEADS):
        locals_.append(
            pltpu.make_async_copy(
                go_hbm.at[:, head * HEAD : (head + 1) * HEAD], go.at[head], local_sem.at[4 + head]
            )
        )
    for copy in locals_:
        copy.start()

    barrier = pltpu.get_barrier_semaphore()
    friends = (right, opposite, left, up, down, twin, beside, following, previous, partner)
    for friend in friends:
        pl.semaphore_signal(barrier, inc=1, device_id=friend, device_id_type=MESH)
    pl.semaphore_wait(barrier, len(friends))

    def rows_of(z_at, core_at):
        return pl.ds(pl.multiple_of(z_at * (2 * part) + core_at * part, 16), part)

    mine = rows_of(z, core)
    only = 1 + 2 * side

    def inject(index, kind, step):
        cols = pl.ds(pl.multiple_of(((col + step) % 4) * width, 128), width)
        at = PLACE[kind] * width
        return remote(
            w_hbm.at[kind, mine, cols], w.at[4 - step, mine, at : at + width],
            inj_send.at[index], inj_recv.at[index], at_col(step),
        )

    pair_injections = [
        inject(index, kind, step)
        for index, (kind, step) in enumerate(((1, 2), (2, 2), (1, 4 - only), (2, 4 - only)))
    ]
    query_injections = [inject(4 + index, 0, step) for index, step in enumerate((2, 1, 3))]

    early_at, late_at = row * half, (1 - row) * half
    early, late = (pl.ds(pl.multiple_of(at, 64), half) for at in (early_at, late_at))
    quarters = [pl.ds(pl.multiple_of(early_at + i * group, 32), group) for i in (0, 1)]

    def own_act(index, way):
        rows = (quarters[way], quarters[1 - way], late)[index]
        return remote(
            act_hbm.at[rows], act.at[3 - 2 * way, rows], act_send.at[way, index], act_recv.at[way, index],
            (right, left)[way],
        )

    def far_act(way):
        rows = quarters[way]
        there = act.at[2, rows]
        return (
            remote(act.at[3 - 2 * way, rows], there, fwd_send.at[way], fwd_recv.at[way], (right, left)[way]),
            remote(there, there, swap_send.at[way], swap_recv.at[way], partner),
        )

    own_acts = [[own_act(index, way) for way in (0, 1)] for index in range(3)]
    far_acts = [far_act(way) for way in (0, 1)]
    for copy in pair_injections + own_acts[0] + query_injections:
        start(copy)

    def pass_on():
        for way in (0, 1):
            own_acts[0][way].wait_recv()
            start(far_acts[way][0])
        for copies in own_acts[1:]:
            for copy in copies:
                start(copy)

    def hand_over():
        for copy, swap in far_acts:
            copy.wait_recv()
            start(swap)

    for copy in locals_[:4]:
        copy.wait()

    @pl.loop(0, 2)
    def _(i):
        rows = pl.ds(pl.multiple_of(i * half, half), half)
        acc[rows, :] = dot(act[0, rows, :], w[0])

    for copy in locals_[4:]:
        copy.wait()
    for head in range(HEADS):
        go_t[head] = jnp.transpose(go[head])

    def ring(way, step):
        origin = (z + n_z - step) % n_z if way == 0 else (z + step) % n_z
        rows = rows_of(origin, core)
        if step < n_z // 2 - 1:
            blocks = [w.at[pl.ds(1 + side, 2), rows, 0 : 2 * width], w.at[1:4, rows, 2 * width : total]]
        elif way == 0:
            blocks = [w.at[2, rows, 0 : 2 * width], w.at[1:3, rows, 2 * width : total]]
        else:
            blocks = [w.at[only, rows, 0 : 2 * width], w.at[3, rows, 2 * width : total]]
        return [
            remote(block, block, z_send.at[way, step, i], z_recv.at[way, step, i], (up, down)[way])
            for i, block in enumerate(blocks)
        ]

    steps = n_z // 2
    origins = [[z]]
    for step in range(1, steps):
        origins.append([(z + n_z - step) % n_z, (z + step) % n_z])
    origins.append([(z + steps) % n_z])

    def spread(index, origin):
        rows = rows_of(origin, core)
        blocks = (w.at[only, rows, 0 : 2 * width], w.at[1:4, rows, 0 : 2 * width], w.at[1:4, rows, 2 * width : total])
        return (
            remote(blocks[0], blocks[0], y_send.at[index], y_recv.at[index], beside),
            remote(blocks[1], blocks[1], core_send.at[0, index], core_recv.at[0, index], twin),
            remote(blocks[2], blocks[2], core_send.at[1, index], core_recv.at[1, index], twin),
        )

    rings = [[ring(way, step) for way in (0, 1)] for step in range(steps)]
    spreads, count = [], 0
    for members in origins:
        spreads.append([spread(count + i, origin) for i, origin in enumerate(members)])
        count += len(members)

    def across_pairs(step):
        for exchange, across, _ in spreads[step]:
            exchange.wait_recv()
            start(across)

    def turn_pairs(step):
        for way in (0, 1):
            if step > 0:
                rings[step - 1][way][0].wait_recv()
            if step < steps:
                start(rings[step][way][0])
                if way < len(spreads[step]):
                    start(spreads[step][way][0])
        if step == steps:
            start(spreads[step][0][0])
        if step > 0:
            across_pairs(step - 1)

    def turn_queries(step):
        for way in (0, 1):
            if step > 0:
                rings[step - 1][way][1].wait_recv()
            if step < steps:
                start(rings[step][way][1])
        for _, _, across in spreads[step]:
            start(across)

    for copy in pair_injections:
        copy.wait_recv()
    turn_pairs(0)
    turn_pairs(1)
    for copy in query_injections:
        copy.wait_recv()
    turn_queries(0)
    pass_on()
    turn_pairs(2)
    turn_queries(1)
    hand_over()
    turn_pairs(3)
    turn_queries(2)
    turn_pairs(4)
    across_pairs(steps)
    turn_queries(3)
    for members in spreads:
        for _, across, _ in members:
            across.wait_recv()

    def keep_pairs(rows, done):
        for head in range(HEADS):
            for kind in range(2):
                at = kind * width + head * HEAD
                pair[head, kind, rows, :] = done[:, at : at + HEAD].astype(BF)

    def keep_queries(rows, done):
        for head in range(HEADS):
            query[head, rows, :] = done[:, head * HEAD : (head + 1) * HEAD].astype(BF)

    def kv_copy(index, heads, rows):
        return remote(
            pair.at[heads, :, rows, :], prior.at[heads, :, rows, :], kv_send.at[index], kv_recv.at[index], following
        )

    kv_copies = [kv_copy(HEADS, pl.ds(0, HEADS), early)]
    kv_copies += [kv_copy(head, pl.ds(head, 1), late) for head in range(HEADS)]
    for copy in own_acts[1]:
        copy.wait_recv()

    def product(rows, cols):
        return acc[rows, cols] + sum(dot(act[index, rows, :], w[index, :, cols]) for index in (1, 2, 3))

    pair_cols, query_cols = pl.ds(0, 2 * width), pl.ds(2 * width, width)
    keep_pairs(early, product(early, pair_cols))
    start(kv_copies[0])
    turn_queries(4)
    for members in spreads:
        for _, _, across in members:
            across.wait_recv()
    keep_queries(early, product(early, query_cols))
    for copy in own_acts[2]:
        copy.wait_recv()
    for _, swap in far_acts:
        swap.wait_recv()
    keep_pairs(late, product(late, pair_cols))
    for copy in kv_copies[1:]:
        start(copy)
    keep_queries(late, product(late, query_cols))
    for head in range(HEADS):
        for kind in range(2):
            pair_t[head, kind] = jnp.transpose(pair[head, kind])

    scaling = HEAD**-0.5
    base = scaling * LOG2E
    has_prior = seq > 0
    tiles = (
        (0, 256, s_a, dp_a, p_a, ds_a),
        (256, 256, s_b, dp_b, p_b, ds_b),
        (512, 128, s_c, dp_c, p_c, ds_c),
    )
    for head in range(HEADS):
        for q0, size, s_own, dp_own, _, _ in tiles:
            seen = q0 + size
            scores = dot_nt(pair[head, 0, 0:seen, :], query[head, q0:seen, :])
            key_at = lax.broadcasted_iota(jnp.int32, (seen, size), 0)
            query_at = lax.broadcasted_iota(jnp.int32, (seen, size), 1) + q0
            s_own[head] = jnp.where(key_at <= query_at, scores, -jnp.inf)
            dp_own[head] = dot_nt(pair[head, 1, 0:seen, :], go[head, q0:seen, :])

    order = [
        pl.ds(pl.multiple_of(at * half + i * group, 32), group) for at in (1 - row, row) for i in range(GROUPS // 2)
    ]
    gr_copies = [
        remote(sent_grad.at[head], back_grad.at[head], gr_send.at[head], gr_recv.at[head], previous)
        for head in range(HEADS - 1)
    ]
    gr_copies += [
        remote(
            sent_grad.at[HEADS - 1, :, rows, :], back_grad.at[HEADS - 1, :, rows, :],
            gr_send.at[HEADS - 1 + i], gr_recv.at[HEADS - 1 + i], previous,
        )
        for i, rows in enumerate(order)
    ]
    for head in range(HEADS):
        if head == 0:
            kv_copies[0].wait_recv()
        kv_copies[1 + head].wait_recv()
        for kind in range(2):
            prior_t[head, kind] = jnp.transpose(prior[head, kind])
        for q0, size, s_own, dp_own, p_own, ds_own in tiles:
            seen = q0 + size
            s_prior = dot_nt(prior[head, 0], query[head, q0:seen, :])
            mine_s = s_own[head]
            top_prior = jnp.where(has_prior, jnp.max(s_prior, axis=0, keepdims=True), -jnp.inf)
            highest = jnp.maximum(jnp.max(mine_s, axis=0, keepdims=True), top_prior) * base
            e_own = jnp.exp2(mine_s * base - highest)
            e_prior = jnp.exp2(s_prior * base - jnp.where(has_prior, highest, jnp.inf))
            inverse = 1.0 / (jnp.sum(e_own, axis=0, keepdims=True) + jnp.sum(e_prior, axis=0, keepdims=True))
            w_own, w_prior = e_own * inverse, e_prior * inverse
            b_own, b_prior = w_own.astype(BF), w_prior.astype(BF)
            p_own[head] = b_own
            p_prior[:, q0:seen] = b_prior
            ctx_t = dot(prior_t[head, 1], b_prior) + dot(pair_t[head, 1, :, 0:seen], b_own)
            delta = jnp.sum(go_t[head, :, q0:seen].astype(F32) * ctx_t, axis=0, keepdims=True)
            attn_ref[q0:seen, head * HEAD : (head + 1) * HEAD] = jnp.transpose(ctx_t).astype(BF)
            ds_own[head] = (w_own * (dp_own[head] - delta)).astype(BF)
            dp_prior = dot_nt(prior[head, 1], go[head, q0:seen, :])
            ds_prior[head, :, q0:seen] = (w_prior * (dp_prior - delta)).astype(BF)
        if head < HEADS - 1:
            sent_grad[head, 0] = (dot(ds_prior[head], query[head]) * scaling).astype(BF)
            sent_grad[head, 1] = dot(p_prior[...], go[head]).astype(BF)
            start(gr_copies[head])
        else:
            for i, rows in enumerate(order):
                sent_grad[head, 0, rows, :] = (dot(ds_prior[head, rows, :], query[head]) * scaling).astype(BF)
                sent_grad[head, 1, rows, :] = dot(p_prior[rows, :], go[head]).astype(BF)
                start(gr_copies[head + i])

    for head in range(HEADS):
        for q0, size, _, _, p_own, ds_own in tiles:
            seen = q0 + size
            dq_t = dot(prior_t[head, 0], ds_prior[head, :, q0:seen]) + dot(pair_t[head, 0, :, 0:seen], ds_own[head])
            at = 2 * width + head * HEAD
            grads[q0:seen, at : at + HEAD] = (jnp.transpose(dq_t) * scaling).astype(BF)
            terms = (dot(ds_own[head], query[head, q0:seen, :]) * scaling, dot(p_own[head], go[head, q0:seen, :]))
            for kind in range(2):
                if q0:
                    own_grad[head, kind, 0:q0, :] = own_grad[head, kind, 0:q0, :] + terms[kind][0:q0]
                own_grad[head, kind, q0:seen, :] = terms[kind][q0:seen]

    mid = depth // 2
    halves = [pl.ds(pl.multiple_of(at * half, half), half) for at in (1 - row, row)]
    pieces = [pl.ds(i * group, group) for i in range(GROUPS // 2)]

    def collect(which):
        if which == 0:
            for head in range(HEADS - 1):
                gr_copies[head].wait_recv()
        for i in range(GROUPS // 2):
            gr_copies[HEADS - 1 + which * (GROUPS // 2) + i].wait_recv()
        rows = halves[which]
        for head in range(HEADS):
            for kind in range(2):
                at = kind * width + head * HEAD
                back = back_grad[head, kind, rows, :].astype(F32)
                grads[rows, at : at + HEAD] = (own_grad[head, kind, rows, :] + back).astype(BF)

    def share(index, which):
        return dot_nt(grads[halves[which], :], w[index])

    cross_copies = [
        remote(cross_out.at[rows], cross_in.at[rows], cross_send.at[i], cross_recv.at[i], partner)
        for i, rows in enumerate(pieces)
    ]
    row_copies = [
        remote(row_out.at[rows], row_in.at[rows], row_send.at[i], row_recv.at[i], partner)
        for i, rows in enumerate(pieces)
    ]
    opp_copies = [
        [
            remote(opp_out.at[way, rows], opp_in.at[way, rows], opp_send.at[way, i], opp_recv.at[way, i], (right, left)[way])
            for i, rows in enumerate(pieces)
        ]
        for way in (0, 1)
    ]
    full_copies = [
        [
            [
                remote(
                    full_out.at[way, which, rows], full_in.at[way, which, rows],
                    full_send.at[way, which, i], full_recv.at[way, which, i], (right, left)[way],
                )
                for i, rows in enumerate(pieces)
            ]
            for which in (0, 1)
        ]
        for way in (0, 1)
    ]

    collect(0)
    for way in (0, 1):
        full_out[way, 0] = share((1, 3)[way], 0).astype(BF)
        for copy in full_copies[way][0]:
            start(copy)
    cross_out[...] = share(2, 0).astype(BF)
    for copy in cross_copies:
        start(copy)
    collect(1)
    term = share(2, 1)
    for i, rows in enumerate(pieces):
        cross_copies[i].wait_recv()
        summed = (term[i * group : (i + 1) * group] + cross_in[rows, :].astype(F32)).astype(BF)
        opp_out[0, rows, :] = summed[:, mid:]
        opp_out[1, rows, :] = summed[:, :mid]
        for way in (0, 1):
            start(opp_copies[way][i])
    terms = [share(1, 1), share(3, 1)]
    for i, rows in enumerate(pieces):
        for way in (0, 1):
            piece = terms[way][i * group : (i + 1) * group]
            opp_copies[way][i].wait_recv()
            arrived = opp_in[way, rows, :].astype(F32)
            low, high = piece[:, :mid], piece[:, mid:]
            if way == 0:
                high = high + arrived
            else:
                low = low + arrived
            full_out[way, 1, rows, :mid] = low.astype(BF)
            full_out[way, 1, rows, mid:] = high.astype(BF)
            start(full_copies[way][1][i])
    term = share(0, 0)
    for i, rows in enumerate(pieces):
        piece = term[i * group : (i + 1) * group]
        for way in (0, 1):
            full_copies[way][0][i].wait_recv()
            piece = piece + full_in[way, 0, rows, :].astype(F32)
        row_out[rows, :] = piece.astype(BF)
        start(row_copies[i])
    term = share(0, 1)
    for i, rows in enumerate(pieces):
        row_copies[i].wait_recv()
        piece = term[i * group : (i + 1) * group] + row_in[rows, :].astype(F32)
        for way in (0, 1):
            full_copies[way][1][i].wait_recv()
            piece = piece + full_in[way, 1, rows, :].astype(F32)
        gin_ref[rows, :] = piece.astype(BF)

    for copy in sent:
        copy.wait_send()


def hand_on(a_ref, b_ref, a_out, b_out, a_held, b_held, sems):
    arrive = [pltpu.make_async_copy(a_ref, a_held, sems.at[0]), pltpu.make_async_copy(b_ref, b_held, sems.at[1])]
    leave = [pltpu.make_async_copy(a_held, a_out, sems.at[2]), pltpu.make_async_copy(b_held, b_out, sems.at[3])]
    for copy in arrive:
        copy.start()
    for copy, following in zip(arrive, leave):
        copy.wait()
        following.start()
    for copy in leave:
        copy.wait()


def on_device(activations, qkv_weight, grad_out):
    length, depth = activations.shape
    width = grad_out.shape[1]
    half = length // 2
    steps = lax.axis_size("seq") // 8
    weights = jnp.transpose(qkv_weight, (1, 0, 2))
    anywhere = pl.BlockSpec(memory_space=pl.ANY)
    vmem = pl.BlockSpec(memory_space=pltpu.VMEM)
    dma = pltpu.SemaphoreType.DMA
    attention, grad_input = pl.pallas_call(
        kernel,
        out_shape=(
            jax.ShapeDtypeStruct((length, width), BF),
            jax.ShapeDtypeStruct((half, depth), BF),
        ),
        in_specs=[anywhere] * 3,
        out_specs=(vmem, vmem),
        scratch_shapes=[
            pltpu.VMEM((4, length, depth), BF),
            pltpu.VMEM((4, depth, 3 * width), BF),
            pltpu.VMEM((length, 3 * width), F32),
            pltpu.VMEM((HEADS, length, HEAD), BF),
            pltpu.VMEM((HEADS, HEAD, length), BF),
            pltpu.VMEM((HEADS, length, HEAD), BF),
            pltpu.VMEM((HEADS, 2, length, HEAD), BF),
            pltpu.VMEM((HEADS, 2, HEAD, length), BF),
            pltpu.VMEM((HEADS, 2, length, HEAD), BF),
            pltpu.VMEM((HEADS, 2, HEAD, length), BF),
            *[pltpu.VMEM((HEADS, *tile), kind) for kind in (F32, F32, BF, BF) for tile in TILES],
            pltpu.VMEM((length, length), BF),
            pltpu.VMEM((HEADS, length, length), BF),
            pltpu.VMEM((HEADS, 2, length, HEAD), F32),
            pltpu.VMEM((HEADS, 2, length, HEAD), BF),
            pltpu.VMEM((HEADS, 2, length, HEAD), BF),
            pltpu.VMEM((length, 3 * width), BF),
            pltpu.VMEM((half, depth), BF),
            pltpu.VMEM((half, depth), BF),
            pltpu.VMEM((2, half, depth // 2), BF),
            pltpu.VMEM((2, half, depth // 2), BF),
            pltpu.VMEM((2, 2, half, depth), BF),
            pltpu.VMEM((2, 2, half, depth), BF),
            pltpu.VMEM((half, depth), BF),
            pltpu.VMEM((half, depth), BF),
            dma((7,)),
            *[dma((7,))] * 2,
            *[dma((2, 3))] * 2,
            *[dma((2,))] * 4,
            *[dma((2, steps, 2))] * 2,
            *[dma((2 * steps,))] * 2,
            *[dma((2, 2 * steps))] * 2,
            *[dma((HEADS + 1,))] * 2,
            *[dma((HEADS - 1 + GROUPS,))] * 2,
            *[dma((GROUPS // 2,))] * 2,
            *[dma((2, GROUPS // 2))] * 2,
            *[dma((2, 2, GROUPS // 2))] * 2,
            *[dma((GROUPS // 2,))] * 2,
        ],
        compiler_params=pltpu.CompilerParams(
            collective_id=0, has_side_effects=True, vmem_limit_bytes=60 * 2**20
        ),
    )(activations, weights, grad_out)
    return pl.pallas_call(
        hand_on,
        out_shape=(
            jax.ShapeDtypeStruct((length, width), BF),
            jax.ShapeDtypeStruct((half, depth), BF),
        ),
        in_specs=[anywhere] * 2,
        out_specs=(anywhere, anywhere),
        scratch_shapes=[pltpu.VMEM((length, width), BF), pltpu.VMEM((half, depth), BF), dma((4,))],
        compiler_params=pltpu.CompilerParams(vmem_limit_bytes=60 * 2**20),
    )(attention, grad_input)


def solution(mesh):
    in_specs = (P("seq", "col"), P("col", None, "row"), P("seq", ("row", "col")))
    out_specs = (P("seq", ("row", "col")), P(("seq", "row"), "col"))
    return jax.shard_map(on_device, mesh=mesh, in_specs=in_specs, out_specs=out_specs, check_vma=False)
```

time: 119 us -> 111 us (0.933)
  Pallas kernels: 114 us -> 110 us
  local copies, waits for them, and re-layouts: 3.7 us -> 0 us
    pallas_call x1, Pallas kernels: 114 us -> 108 us  [on_device(): pl.pallas_call(kernel, out_shape=(jax.ShapeDtypeStruct((length, width), B...]
    unnamed x2 -> x0, local copies, waits for them, and re-layouts: 3.7 us -> none
    pallas_call x0 -> x1, Pallas kernels: none -> 2 us  [on_device(): pl.pallas_call(hand_on, out_shape=(jax.ShapeDtypeStruct((length, width),...]
where the time goes in v2:
time: 111 us; the launch traced here: 110 us
  Pallas kernels  110 us (99%)
    pallas_call x1, Pallas kernels, on_device(): pl.pallas_call(kernel, out_shape=(jax.ShapeDtypeStruct((length, width), B...  108 us

profile of v2, /device:TPU:1, one launch (start us, length us, event | category | flops | bytes accessed | tf_op | source)
XLA Modules:
  0.0 110.4 jit_solution(4347535561618562991)
XLA Ops:
  0.6 107.6 %shard_map.50 = (bf16[640,384]{1,0:T(8,128)(2,1)}, bf16[320,768]{1,0:T(8,128)(2,1)}) custom-call(bf16[640,768]{1,0:T(8,128)(2,1)} %act_hbm.1, bf16[3,768,1536]{2,1,0:T(8,128)(2,1)} %bitcast.1, bf16[640,384]{1,0:T(8,128)(2,1)} %go_hbm.1), custom_call_target="tpu_custom_call" | custom-call | tf_op jit(solution)/shard_map/pallas_call | solution.py:489
  108.2 2.0 %shard_map.51 = (bf16[640,384]{1,0:T(8,128)(2,1)}, bf16[320,768]{1,0:T(8,128)(2,1)}) custom-call(bf16[640,384]{1,0:T(8,128)(2,1)} %get-tuple-element.4.a_ref, bf16[320,768]{1,0:T(8,128)(2,1)} %get-tuple-element.5.b_ref), custom_call_target="tpu_custom_call" | custom-call | tf_op jit(solution)/shard_map/pallas_call | solution.py:541

commit v3 on v2

--- a/solution.py
+++ b/solution.py
@@ -29,7 +29,7 @@
 def kernel(
     act_hbm, w_hbm, go_hbm, attn_ref, gin_ref,
     act, w, acc, go, go_t, query, pair, pair_t, prior, prior_t,
-    s_a, s_b, s_c, dp_a, dp_b, dp_c, p_a, p_b, p_c, ds_a, ds_b, ds_c, p_prior, ds_prior,
+    stats, e_a, e_b, e_c, dp_a, dp_b, dp_c, p_a, p_b, p_c, ds_a, ds_b, ds_c, p_prior, ds_prior,
     own_grad, sent_grad, back_grad, grads, cross_out, cross_in, opp_out, opp_in, full_out, full_in, row_out, row_in,
     local_sem, inj_send, inj_recv, act_send, act_recv, fwd_send, fwd_recv, swap_send, swap_recv,
     z_send, z_recv, y_send, y_recv, core_send, core_recv, kv_send, kv_recv, gr_send, gr_recv,
@@ -107,9 +107,9 @@
 
     pair_injections = [
         inject(index, kind, step)
-        for index, (kind, step) in enumerate(((1, 2), (2, 2), (1, 4 - only), (2, 4 - only)))
-    ]
-    query_injections = [inject(4 + index, 0, step) for index, step in enumerate((2, 1, 3))]
+        for index, (kind, step) in enumerate(((1, 2), (2, 2), (1, 1), (2, 1), (1, 3), (2, 3)))
+    ]
+    query_injections = [inject(6 + index, 0, step) for index, step in enumerate((2, 1, 3))]
 
     early_at, late_at = row * half, (1 - row) * half
     early, late = (pl.ds(pl.multiple_of(at, 64), half) for at in (early_at, late_at))
@@ -165,11 +165,11 @@
         origin = (z + n_z - step) % n_z if way == 0 else (z + step) % n_z
         rows = rows_of(origin, core)
         if step < n_z // 2 - 1:
-            blocks = [w.at[pl.ds(1 + side, 2), rows, 0 : 2 * width], w.at[1:4, rows, 2 * width : total]]
+            blocks = [w.at[1:4, rows, 0 : 2 * width], w.at[1:4, rows, 2 * width : total]]
         elif way == 0:
-            blocks = [w.at[2, rows, 0 : 2 * width], w.at[1:3, rows, 2 * width : total]]
+            blocks = [w.at[1:4, rows, 0:width], w.at[1:3, rows, 2 * width : total]]
         else:
-            blocks = [w.at[only, rows, 0 : 2 * width], w.at[3, rows, 2 * width : total]]
+            blocks = [w.at[1:4, rows, width : 2 * width], w.at[3, rows, 2 * width : total]]
         return [
             remote(block, block, z_send.at[way, step, i], z_recv.at[way, step, i], (up, down)[way])
             for i, block in enumerate(blocks)
@@ -198,7 +198,6 @@
 
     def across_pairs(step):
         for exchange, across, _ in spreads[step]:
-            exchange.wait_recv()
             start(across)
 
     def turn_pairs(step):
@@ -207,10 +206,6 @@
                 rings[step - 1][way][0].wait_recv()
             if step < steps:
                 start(rings[step][way][0])
-                if way < len(spreads[step]):
-                    start(spreads[step][way][0])
-        if step == steps:
-            start(spreads[step][0][0])
         if step > 0:
             across_pairs(step - 1)
 
@@ -269,11 +264,6 @@
     pair_cols, query_cols = pl.ds(0, 2 * width), pl.ds(2 * width, width)
     keep_pairs(early, product(early, pair_cols))
     start(kv_copies[0])
-    turn_queries(4)
-    for members in spreads:
-        for _, _, across in members:
-            across.wait_recv()
-    keep_queries(early, product(early, query_cols))
     for copy in own_acts[2]:
         copy.wait_recv()
     for _, swap in far_acts:
@@ -281,7 +271,12 @@
     keep_pairs(late, product(late, pair_cols))
     for copy in kv_copies[1:]:
         start(copy)
-    keep_queries(late, product(late, query_cols))
+    turn_queries(4)
+    for members in spreads:
+        for _, _, across in members:
+            across.wait_recv()
+    for rows in (early, late):
+        keep_queries(rows, product(rows, query_cols))
     for head in range(HEADS):
         for kind in range(2):
             pair_t[head, kind] = jnp.transpose(pair[head, kind])
@@ -290,17 +285,22 @@
     base = scaling * LOG2E
     has_prior = seq > 0
     tiles = (
-        (0, 256, s_a, dp_a, p_a, ds_a),
-        (256, 256, s_b, dp_b, p_b, ds_b),
-        (512, 128, s_c, dp_c, p_c, ds_c),
+        (0, 256, e_a, dp_a, p_a, ds_a),
+        (256, 256, e_b, dp_b, p_b, ds_b),
+        (512, 128, e_c, dp_c, p_c, ds_c),
     )
     for head in range(HEADS):
-        for q0, size, s_own, dp_own, _, _ in tiles:
+        for q0, size, e_own, dp_own, _, _ in tiles:
             seen = q0 + size
             scores = dot_nt(pair[head, 0, 0:seen, :], query[head, q0:seen, :])
             key_at = lax.broadcasted_iota(jnp.int32, (seen, size), 0)
             query_at = lax.broadcasted_iota(jnp.int32, (seen, size), 1) + q0
-            s_own[head] = jnp.where(key_at <= query_at, scores, -jnp.inf)
+            scores = jnp.where(key_at <= query_at, scores, -jnp.inf) * base
+            highest = jnp.max(scores, axis=0, keepdims=True)
+            raised = jnp.exp2(scores - highest)
+            e_own[head] = raised
+            stats[head, 0:1, q0:seen] = highest
+            stats[head, 1:2, q0:seen] = jnp.sum(raised, axis=0, keepdims=True)
             dp_own[head] = dot_nt(pair[head, 1, 0:seen, :], go[head, q0:seen, :])
 
     order = [
@@ -323,16 +323,16 @@
         kv_copies[1 + head].wait_recv()
         for kind in range(2):
             prior_t[head, kind] = jnp.transpose(prior[head, kind])
-        for q0, size, s_own, dp_own, p_own, ds_own in tiles:
+        for q0, size, e_own, dp_own, p_own, ds_own in tiles:
             seen = q0 + size
             s_prior = dot_nt(prior[head, 0], query[head, q0:seen, :])
-            mine_s = s_own[head]
-            top_prior = jnp.where(has_prior, jnp.max(s_prior, axis=0, keepdims=True), -jnp.inf)
-            highest = jnp.maximum(jnp.max(mine_s, axis=0, keepdims=True), top_prior) * base
-            e_own = jnp.exp2(mine_s * base - highest)
+            own_top, own_sum = stats[head, 0:1, q0:seen], stats[head, 1:2, q0:seen]
+            prior_top = jnp.where(has_prior, jnp.max(s_prior, axis=0, keepdims=True) * base, -jnp.inf)
+            highest = jnp.maximum(own_top, prior_top)
             e_prior = jnp.exp2(s_prior * base - jnp.where(has_prior, highest, jnp.inf))
-            inverse = 1.0 / (jnp.sum(e_own, axis=0, keepdims=True) + jnp.sum(e_prior, axis=0, keepdims=True))
-            w_own, w_prior = e_own * inverse, e_prior * inverse
+            shrink = jnp.exp2(own_top - highest)
+            inverse = 1.0 / (own_sum * shrink + jnp.sum(e_prior, axis=0, keepdims=True))
+            w_own, w_prior = e_own[head] * (shrink * inverse), e_prior * inverse
             b_own, b_prior = w_own.astype(BF), w_prior.astype(BF)
             p_own[head] = b_own
             p_prior[:, q0:seen] = b_prior
@@ -505,6 +505,7 @@
             pltpu.VMEM((HEADS, 2, HEAD, length), BF),
             pltpu.VMEM((HEADS, 2, length, HEAD), BF),
             pltpu.VMEM((HEADS, 2, HEAD, length), BF),
+            pltpu.VMEM((HEADS, 2, length), F32),
             *[pltpu.VMEM((HEADS, *tile), kind) for kind in (F32, F32, BF, BF) for tile in TILES],
             pltpu.VMEM((length, length), BF),
             pltpu.VMEM((HEADS, length, length), BF),
@@ -521,7 +522,7 @@
             pltpu.VMEM((half, depth), BF),
             pltpu.VMEM((half, depth), BF),
             dma((7,)),
-            *[dma((7,))] * 2,
+            *[dma((9,))] * 2,
             *[dma((2, 3))] * 2,
             *[dma((2,))] * 4,
             *[dma((2, steps, 2))] * 2,

time: 111 us -> 107 us (0.964)
  Pallas kernels: 110 us -> 106 us
    pallas_call x1, Pallas kernels: 108 us -> 104 us  [on_device(): pl.pallas_call(kernel, out_shape=(jax.ShapeDtypeStruct((length, width), B...]
where the time goes in v3:
time: 107 us
  Pallas kernels  106 us (99%)
    pallas_call x1, Pallas kernels, on_device(): pl.pallas_call(kernel, out_shape=(jax.ShapeDtypeStruct((length, width), B...  104 us

profile of v3, /device:TPU:1, one launch (start us, length us, event | category | flops | bytes accessed | tf_op | source)
XLA Modules:
  0.0 106.8 jit_solution(10618976923515933924)
XLA Ops:
  0.6 103.9 %shard_map.50 = (bf16[640,384]{1,0:T(8,128)(2,1)}, bf16[320,768]{1,0:T(8,128)(2,1)}) custom-call(bf16[640,768]{1,0:T(8,128)(2,1)} %act_hbm.1, bf16[3,768,1536]{2,1,0:T(8,128)(2,1)} %bitcast.1, bf16[640,384]{1,0:T(8,128)(2,1)} %go_hbm.1), custom_call_target="tpu_custom_call" | custom-call | tf_op jit(solution)/shard_map/pallas_call | solution.py:489
  104.6 2.0 %shard_map.51 = (bf16[640,384]{1,0:T(8,128)(2,1)}, bf16[320,768]{1,0:T(8,128)(2,1)}) custom-call(bf16[640,384]{1,0:T(8,128)(2,1)} %get-tuple-element.4.a_ref, bf16[320,768]{1,0:T(8,128)(2,1)} %get-tuple-element.5.b_ref), custom_call_target="tpu_custom_call" | custom-call | tf_op jit(solution)/shard_map/pallas_call | solution.py:542

commit v4 on v3

--- a/solution.py
+++ b/solution.py
@@ -32,13 +32,13 @@
     stats, e_a, e_b, e_c, dp_a, dp_b, dp_c, p_a, p_b, p_c, ds_a, ds_b, ds_c, p_prior, ds_prior,
     own_grad, sent_grad, back_grad, grads, cross_out, cross_in, opp_out, opp_in, full_out, full_in, row_out, row_in,
     local_sem, inj_send, inj_recv, act_send, act_recv, fwd_send, fwd_recv, swap_send, swap_recv,
-    z_send, z_recv, y_send, y_recv, core_send, core_recv, kv_send, kv_recv, gr_send, gr_recv,
+    z_send, z_recv, core_send, core_recv, kv_send, kv_recv, gr_send, gr_recv,
     cross_send, cross_recv, opp_send, opp_recv, full_send, full_recv, row_send, row_recv,
 ):
     seq, row, col = lax.axis_index("seq"), lax.axis_index("row"), lax.axis_index("col")
     n_seq = lax.axis_size("seq")
     n_z = n_seq // 4
-    z, side, core = seq // 4, (seq // 2) % 2, seq % 2
+    z, core = seq // 4, seq % 2
     length, depth = act_hbm.shape
     width = go_hbm.shape[1]
     total = 3 * width
@@ -55,7 +55,6 @@
     right, opposite, left = at_col(1), at_col(2), at_col(3)
     up, down = at_seq((seq + 4) % n_seq), at_seq((seq + n_seq - 4) % n_seq)
     twin = at_seq(seq + 1 - 2 * core)
-    beside = at_seq(seq + 2 - 4 * side)
     following, previous = at_seq((seq + 1) % n_seq), at_seq((seq + n_seq - 1) % n_seq)
     partner = (seq, 1 - row, col)
     sent = []
@@ -86,7 +85,7 @@
         copy.start()
 
     barrier = pltpu.get_barrier_semaphore()
-    friends = (right, opposite, left, up, down, twin, beside, following, previous, partner)
+    friends = (right, opposite, left, up, down, twin, following, previous, partner)
     for friend in friends:
         pl.semaphore_signal(barrier, inc=1, device_id=friend, device_id_type=MESH)
     pl.semaphore_wait(barrier, len(friends))
@@ -95,21 +94,20 @@
         return pl.ds(pl.multiple_of(z_at * (2 * part) + core_at * part, 16), part)
 
     mine = rows_of(z, core)
-    only = 1 + 2 * side
-
-    def inject(index, kind, step):
+
+    def inject(index, kind, step, rows):
         cols = pl.ds(pl.multiple_of(((col + step) % 4) * width, 128), width)
         at = PLACE[kind] * width
         return remote(
-            w_hbm.at[kind, mine, cols], w.at[4 - step, mine, at : at + width],
+            w_hbm.at[kind, rows, cols], w.at[4 - step, rows, at : at + width],
             inj_send.at[index], inj_recv.at[index], at_col(step),
         )
 
-    pair_injections = [
-        inject(index, kind, step)
-        for index, (kind, step) in enumerate(((1, 2), (2, 2), (1, 1), (2, 1), (1, 3), (2, 3)))
-    ]
-    query_injections = [inject(6 + index, 0, step) for index, step in enumerate((2, 1, 3))]
+    kinds_steps = ((1, 2), (2, 2), (1, 1), (2, 1), (1, 3), (2, 3))
+    across_z = rows_of((z + n_z // 2) % n_z, core)
+    pair_injections = [inject(index, *member, mine) for index, member in enumerate(kinds_steps)]
+    far_injections = [inject(6 + index, *member, across_z) for index, member in enumerate(kinds_steps)]
+    query_injections = [inject(12 + index, 0, step, mine) for index, step in enumerate((2, 1, 3))]
 
     early_at, late_at = row * half, (1 - row) * half
     early, late = (pl.ds(pl.multiple_of(at, 64), half) for at in (early_at, late_at))
@@ -139,9 +137,8 @@
         for way in (0, 1):
             own_acts[0][way].wait_recv()
             start(far_acts[way][0])
-        for copies in own_acts[1:]:
-            for copy in copies:
-                start(copy)
+        for copy in own_acts[1] + far_injections + own_acts[2]:
+            start(copy)
 
     def hand_over():
         for copy, swap in far_acts:
@@ -166,12 +163,11 @@
         rows = rows_of(origin, core)
         if step < n_z // 2 - 1:
             blocks = [w.at[1:4, rows, 0 : 2 * width], w.at[1:4, rows, 2 * width : total]]
-        elif way == 0:
-            blocks = [w.at[1:4, rows, 0:width], w.at[1:3, rows, 2 * width : total]]
         else:
-            blocks = [w.at[1:4, rows, width : 2 * width], w.at[3, rows, 2 * width : total]]
+            blocks = [None, w.at[1:3, rows, 2 * width : total] if way == 0 else w.at[3, rows, 2 * width : total]]
         return [
             remote(block, block, z_send.at[way, step, i], z_recv.at[way, step, i], (up, down)[way])
+            if block is not None else None
             for i, block in enumerate(blocks)
         ]
 
@@ -183,12 +179,10 @@
 
     def spread(index, origin):
         rows = rows_of(origin, core)
-        blocks = (w.at[only, rows, 0 : 2 * width], w.at[1:4, rows, 0 : 2 * width], w.at[1:4, rows, 2 * width : total])
-        return (
-            remote(blocks[0], blocks[0], y_send.at[index], y_recv.at[index], beside),
-            remote(blocks[1], blocks[1], core_send.at[0, index], core_recv.at[0, index], twin),
-            remote(blocks[2], blocks[2], core_send.at[1, index], core_recv.at[1, index], twin),
-        )
+        blocks = (w.at[1:4, rows, 0 : 2 * width], w.at[1:4, rows, 2 * width : total])
+        return [
+            remote(block, block, core_send.at[i, index], core_recv.at[i, index], twin) for i, block in enumerate(blocks)
+        ]
 
     rings = [[ring(way, step) for way in (0, 1)] for step in range(steps)]
     spreads, count = [], 0
@@ -197,14 +191,14 @@
         count += len(members)
 
     def across_pairs(step):
-        for exchange, across, _ in spreads[step]:
+        for across, _ in spreads[step]:
             start(across)
 
     def turn_pairs(step):
         for way in (0, 1):
             if step > 0:
                 rings[step - 1][way][0].wait_recv()
-            if step < steps:
+            if step < steps - 1:
                 start(rings[step][way][0])
         if step > 0:
             across_pairs(step - 1)
@@ -215,7 +209,7 @@
                 rings[step - 1][way][1].wait_recv()
             if step < steps:
                 start(rings[step][way][1])
-        for _, _, across in spreads[step]:
+        for _, across in spreads[step]:
             start(across)
 
     for copy in pair_injections:
@@ -231,11 +225,13 @@
     hand_over()
     turn_pairs(3)
     turn_queries(2)
-    turn_pairs(4)
+    across_pairs(3)
+    for copy in far_injections:
+        copy.wait_recv()
     across_pairs(steps)
     turn_queries(3)
     for members in spreads:
-        for _, across, _ in members:
+        for across, _ in members:
             across.wait_recv()
 
     def keep_pairs(rows, done):
@@ -273,7 +269,7 @@
         start(copy)
     turn_queries(4)
     for members in spreads:
-        for _, _, across in members:
+        for _, across in members:
             across.wait_recv()
     for rows in (early, late):
         keep_queries(rows, product(rows, query_cols))
@@ -522,11 +518,10 @@
             pltpu.VMEM((half, depth), BF),
             pltpu.VMEM((half, depth), BF),
             dma((7,)),
-            *[dma((9,))] * 2,
+            *[dma((15,))] * 2,
             *[dma((2, 3))] * 2,
             *[dma((2,))] * 4,
             *[dma((2, steps, 2))] * 2,
-            *[dma((2 * steps,))] * 2,
             *[dma((2, 2 * steps))] * 2,
             *[dma((HEADS + 1,))] * 2,
             *[dma((HEADS - 1 + GROUPS,))] * 2,

time: 107 us -> 105 us (0.981)
  Pallas kernels: 106 us -> 104 us
    pallas_call x1, Pallas kernels: 104 us -> 102 us  [on_device(): pl.pallas_call(kernel, out_shape=(jax.ShapeDtypeStruct((length, width), B...]
where the time goes in v4:
time: 105 us; the launch traced here: 104 us
  Pallas kernels  104 us (99%)
    pallas_call x1, Pallas kernels, on_device(): pl.pallas_call(kernel, out_shape=(jax.ShapeDtypeStruct((length, width), B...  102 us

profile of v4, /device:TPU:1, one launch (start us, length us, event | category | flops | bytes accessed | tf_op | source)
XLA Modules:
  0.0 104.3 jit_solution(1807608805381543049)
XLA Ops:
  0.6 101.5 %shard_map.50 = (bf16[640,384]{1,0:T(8,128)(2,1)}, bf16[320,768]{1,0:T(8,128)(2,1)}) custom-call(bf16[640,768]{1,0:T(8,128)(2,1)} %act_hbm.1, bf16[3,768,1536]{2,1,0:T(8,128)(2,1)} %bitcast.1, bf16[640,384]{1,0:T(8,128)(2,1)} %go_hbm.1), custom_call_target="tpu_custom_call" | custom-call | tf_op jit(solution)/shard_map/pallas_call | solution.py:485
  102.2 2.0 %shard_map.51 = (bf16[640,384]{1,0:T(8,128)(2,1)}, bf16[320,768]{1,0:T(8,128)(2,1)}) custom-call(bf16[640,384]{1,0:T(8,128)(2,1)} %get-tuple-element.4.a_ref, bf16[320,768]{1,0:T(8,128)(2,1)} %get-tuple-element.5.b_ref), custom_call_target="tpu_custom_call" | custom-call | tf_op jit(solution)/shard_map/pallas_call | solution.py:537
